TPU v7x, 512 devices: a whole 4x8x8 slice. The times are simulated.
512 devices in a mesh: tok: 16 (over x_lo, z), tp: 32 (over y, x_hi, core).
Axes of the slice: x: 4 (x_hi: 2, x_lo: 2; x = x_hi * 2 + x_lo), y: 8, z: 8, core: 2. Of those that a mesh axis runs over, the one named last changes fastest.
Arguments:
- activations: bfloat16 [12288, 4096], P('tok', 'tp'), may hold values from -16 to 16, as said below
- gradients: bfloat16 [12288, 4096], P('tok', 'tp'), may hold values from -16 to 16, as said below
Outputs:
- act_cov: float32 [4096, 4096], P('tp', 'tok')
- grad_cov: float32 [4096, 4096], P('tp', 'tok')
Inputs may be any that keep to these rules, and one draw needn't show every extreme that they name: `activations`: Real-valued entries of order one. `gradients`: Real-valued entries of order one.
All inputs are finite; a program needn't handle non-finite values.
Results may differ from a plain program's by a relative error of at most 0.0003.
Values may be sent and summed in bfloat16 or wider, within the bound.
A program may use at most 64 MiB of HBM per device.

v0:
```python
import jax
import jax.numpy as jnp
from jax import lax
from jax.sharding import PartitionSpec as P


def cross(left, right):
    return lax.dot_general(
        left, right, (((0,), (0,)), ((), ())), preferred_element_type=jnp.float32
    )


def per_device(activations, gradients):
    rows_here = activations.shape[0]
    new_a = cross(activations, lax.all_gather(activations, "tp", axis=1, tiled=True))
    new_g = cross(gradients, lax.all_gather(gradients, "tp", axis=1, tiled=True))
    summed_a, summed_g = (
        lax.psum_scatter(new_a, "tok", scatter_dimension=1, tiled=True),
        lax.psum_scatter(new_g, "tok", scatter_dimension=1, tiled=True),
    )
    scale = jnp.float32(rows_here * lax.axis_size("tok"))
    return (summed_a / scale, summed_g / scale)


def solution(mesh):
    placed = (P("tok", "tp"), P("tok", "tp"))
    return jax.shard_map(
        per_device,
        mesh=mesh,
        in_specs=placed,
        out_specs=(P("tp", "tok"), P("tp", "tok")),
        check_vma=False,
    )
```

profile of v0, /device:TPU:8, one launch (start us, length us, event | category | flops | bytes accessed | tf_op | source)
XLA Modules:
  0.0 382.9 jit_solution(17771866505654631288)
XLA Ops:
  7.2 0.0 all-gather.3.cloned.1.call-start
  7.2 0.7 all-gather.3.cloned.1.call-update
  7.9 0.0 all-gather.5.cloned.1.call-start
  7.9 0.7 all-gather.5.cloned.1.call-update
  8.6 0.0 copy-start
  8.7 0.0 reduce-scatter.3.cloned.1.call-start
  8.7 109.9 %all-gather.3.cloned.1.call-done = bf16[768,4096]{1,0:T(8,128)(2,1)} async-done(((bf16[768,128]{1,0:T(8,128)(2,1)}), bf16[768,4096]{1,0:T(8,128)(2,1)}) %all-gather.3.cloned.1.call-update) | async-done | bytes 6291472 | tf_op jit(solution)/shard_map/all_gather | solution.py:15
  118.6 5.2 %fusion = f32[128,4096]{1,0:T(8,128)} fusion(bf16[768,128]{1,0:T(8,128)(2,1)} %param.2, bf16[768,4096]{1,0:T(8,128)(2,1)} %all-gather.3.cloned.1.call-done), kind=kOutput, calls=%fused_computation.2 | convolution fusion | flops 805306368 | bytes 8585216 | tf_op jit(solution)/shard_map/dot_general | solution.py:8
  123.9 0.0 reduce-scatter.3.cloned.1.call-update
  123.9 0.0 reduce-scatter.5.cloned.1.call-start
  123.9 97.5 %all-gather.5.cloned.1.call-done = bf16[768,4096]{1,0:T(8,128)(2,1)} async-done(((bf16[768,128]{1,0:T(8,128)(2,1)}), bf16[768,4096]{1,0:T(8,128)(2,1)}) %all-gather.5.cloned.1.call-update) | async-done | bytes 6291472 | tf_op jit(solution)/shard_map/all_gather | solution.py:16
  221.4 0.0 copy-done
  221.4 5.2 %fusion.1 = f32[128,4096]{1,0:T(8,128)} fusion(bf16[768,128]{1,0:T(8,128)(2,1)S(1)} %copy-done, bf16[768,4096]{1,0:T(8,128)(2,1)} %all-gather.5.cloned.1.call-done), kind=kOutput, calls=%fused_computation.3 | convolution fusion | flops 805306368 | bytes 8585216 | tf_op jit(solution)/shard_map/dot_general | solution.py:8
  226.6 0.0 reduce-scatter.5.cloned.1.call-update
  226.6 72.3 %reduce-scatter.3.cloned.1.call-done = f32[128,256]{1,0:T(8,128)} async-done(((f32[128,4096]{1,0:T(8,128)}), f32[128,256]{1,0:T(8,128)}) %reduce-scatter.3.cloned.1.call-update) | async-done | bytes 131088 | tf_op jit(solution)/shard_map/reduce_scatter | solution.py:18
  298.9 1.6 broadcast_multiply_fusion.1
  300.4 74.4 %reduce-scatter.5.cloned.1.call-done = f32[128,256]{1,0:T(8,128)} async-done(((f32[128,4096]{1,0:T(8,128)}), f32[128,256]{1,0:T(8,128)}) %reduce-scatter.5.cloned.1.call-update) | async-done | bytes 131088 | tf_op jit(solution)/shard_map/reduce_scatter | solution.py:19
  374.8 1.6 broadcast_multiply_fusion
Async XLA Ops:
  7.2 111.5 %all-gather.3.cloned.1.call-start = ((), (), s32[]{:S(2)}) async-start(), calls=%async_computation.2 | async-start | bytes 6488064 | tf_op jit(solution)/shard_map/all_gather | solution.py:15
  7.9 213.5 %all-gather.5.cloned.1.call-start = ((), (), s32[]{:S(2)}) async-start(), calls=%async_computation.4 | async-start | bytes 6488064 | tf_op jit(solution)/shard_map/all_gather | solution.py:16
  8.6 212.8 %copy-start = (bf16[768,128]{1,0:T(8,128)(2,1)S(1)}, bf16[768,128]{1,0:T(8,128)(2,1)}, u32[]{:S(2)}) copy-start(bf16[768,128]{1,0:T(8,128)(2,1)} %param.3) | copy-start | bytes 589828
  8.7 290.2 %reduce-scatter.3.cloned.1.call-start = ((), (), s32[]{:S(2)}) async-start(), calls=%async_computation.3 | async-start | bytes 2228224 | tf_op jit(solution)/shard_map/reduce_scatter | solution.py:18
  123.9 251.0 %reduce-scatter.5.cloned.1.call-start = ((), (), s32[]{:S(2)}) async-start(), calls=%async_computation.5 | async-start | bytes 2228224 | tf_op jit(solution)/shard_map/reduce_scatter | solution.py:19
Sparse Core Ops, SparseCore 0:
  11.1 107.4 all-gather.2
  121.8 99.5 all-gather.4
  224.2 74.5 reduce-scatter.2
  301.5 73.2 reduce-scatter.4
where the time goes:
time: 383 us
  waiting for transfers between devices  355 us (93%)
  between operations  13.8 us (4%)
  matrix products  10.4 us (3%)
    all_gather x1, waiting for transfers between devices, per_device(): lax.all_gather(activations, 'tp', axis=1, tiled=True)  110 us
    all_gather x1, waiting for transfers between devices, per_device(): lax.all_gather(gradients, 'tp', axis=1, tiled=True)  97.5 us
    reduce_scatter x1, waiting for transfers between devices, per_device(): lax.psum_scatter(new_g, 'tok', scatter_dimension=1, tiled=True)  74.4 us
    reduce_scatter x1, waiting for transfers between devices, per_device(): lax.psum_scatter(new_a, 'tok', scatter_dimension=1, tiled=True)  72.3 us
    dot_general x2, matrix products, cross(): lax.dot_general(left, right, (((0,), (0,)), ((), ())), preferred_element_...  10.4 us
  transfers between devices with their start and end apart: 4, of which 4 were waited for; matrix products, arithmetic and copies ran while one was open for 3% of the time, Pallas kernels for 0%

commit v1 on v0

v1 whole, which is shorter than its diff:
```python
import jax
import jax.numpy as jnp
from jax import lax
from jax.experimental import pallas as pl
from jax.experimental.pallas import tpu as pltpu
from jax.sharding import PartitionSpec as P

TOKENS = 768
WIDE = 128
Y = 8
Z = 8


def place(y, h, core, low, z):
    return (low * Z + z, (y * 2 + h) * 2 + core)


def kernel(
    act, grad, out_a, out_g,
    own, turned, ring, part, part4, zbuf, zbuf4, direct, mirror,
    send_x, recv_x, send_y, recv_y, send_z, recv_z, send_d, recv_d,
):
    tok, tp = lax.axis_index("tok"), lax.axis_index("tp")
    low, z = lax.div(tok, Z), lax.rem(tok, Z)
    y, h, core = lax.div(tp, 4), lax.rem(lax.div(tp, 2), 2), lax.rem(tp, 2)
    x = 2 * h + low

    def remote(src, dst, send, recv, device):
        return pltpu.make_async_remote_copy(
            src_ref=src, dst_ref=dst, send_sem=send, recv_sem=recv,
            device_id=device, device_id_type=pl.DeviceIdType.MESH,
        )

    def at_x(xx, cc):
        return place(y, lax.div(xx, 2), cc, lax.rem(xx, 2), z)

    x_up, x_down = lax.rem(x + 1, 4), lax.rem(x + 3, 4)
    y_up, y_down = lax.rem(y + 1, Y), lax.rem(y + Y - 1, Y)
    z_up, z_down = lax.rem(z + 1, Z), lax.rem(z + Z - 1, Z)
    sibling = place(y, h, 1 - core, low, z)

    barrier = pltpu.get_barrier_semaphore()
    partners = [sibling]
    partners += [at_x(xx, cc) for xx in (x_up, x_down) for cc in (0, 1)]
    partners += [place(yy, h, core, low, z) for yy in (y_up, y_down)]
    partners += [place(y, h, core, low, zz) for zz in (z_up, z_down)]
    for partner in partners:
        pl.semaphore_signal(
            barrier, inc=1, device_id=partner, device_id_type=pl.DeviceIdType.MESH
        )
    pl.semaphore_wait(barrier, len(partners))

    sends = []
    quarter = 2 * h + core
    slot, slot_sem = own.at[low, quarter], recv_x.at[low, quarter]
    for i, ref in enumerate((act, grad)):
        keep = pltpu.make_async_copy(ref, slot, slot_sem)
        give = remote(ref, slot, send_x.at[0], slot_sem, sibling)
        pl.when(core == i)(keep.start)
        pl.when(core != i)(give.start)
    sends.append(remote(act, slot, send_x.at[0], slot_sem, sibling))
    pair = 2 * h + 1 - low
    other = lax.rem(x + 3 + 2 * low, 4)
    first = jnp.where(core == low, other, pair)
    second = jnp.where(core == low, pair, other)
    for n, xx in enumerate((first, second)):
        for i, ref in enumerate((act, grad)):
            copy = remote(ref, slot, send_x.at[1 + 2 * n + i], slot_sem, at_x(xx, i))
            copy.start()
            sends.append(copy)

    def arrive(lo, q):
        pltpu.make_async_copy(own.at[lo, q], own.at[lo, q], recv_x.at[lo, q]).wait()

    def turn(lo, q):
        turned[lo, q] = own[lo, q].T

    def pass_on(source, k, xx, n):
        hh, lo = lax.div(source, 2), lax.rem(source, 2)
        ref = own.at[lo, 2 * hh + k]
        copy = remote(ref, ref, send_x.at[n], recv_x.at[lo, 2 * hh + k], at_x(xx, core))
        copy.start()
        sends.append(copy)

    q = 2 * h + low
    y_next = jnp.where(core == 0, y_down, y_up)
    halves = (low, 1 - low)

    def ring_send(step, n):
        lo = halves[n]
        src = own.at[lo, q] if step == 0 else ring.at[step - 1, lo]
        copy = remote(
            src, ring.at[step, lo], send_y.at[step, n], recv_y.at[step, lo],
            place(y_next, h, core, low, z),
        )
        copy.start()
        sends.append(copy)

    def ring_wait(step, n):
        ref = ring.at[step, halves[n]]
        pltpu.make_async_copy(ref, ref, recv_y.at[step, halves[n]]).wait()

    up_h, up_lo = lax.div(x_up, 2), lax.rem(x_up, 2)
    down_h, down_lo = lax.div(x_down, 2), lax.rem(x_down, 2)
    far = lax.rem(x + 2, 4)
    far_h, far_lo = lax.div(far, 2), lax.rem(far, 2)

    arrive(low, q)
    ring_send(0, 0)
    arrive(1 - low, q)
    ring_send(0, 1)
    arrive(low, 2 * h + 1 - low)
    turn(low, q)
    turn(low, 2 * h + 1 - low)
    ring_wait(0, 0)
    ring_send(1, 0)
    arrive(down_lo, 2 * down_h)
    pass_on(x_down, 0, x_up, 5)
    arrive(up_lo, 2 * up_h + 1)
    pass_on(x_up, 1, x_down, 6)
    ring_wait(0, 1)
    ring_send(1, 1)
    turn(down_lo, 2 * down_h)
    turn(up_lo, 2 * up_h + 1)
    ring_wait(1, 0)
    ring_send(2, 0)
    arrive(lax.rem(other, 2), 2 * lax.div(other, 2) + 1 - low)
    turn(down_lo, 2 * down_h + 1)
    turn(up_lo, 2 * up_h)
    ring_wait(1, 1)
    ring_send(2, 1)
    for k in (0, 1):
        arrive(far_lo, 2 * far_h + k)
        turn(far_lo, 2 * far_h + k)

    a4 = jnp.where(y < Y // 2, h, 1 - h)

    def product(d):
        def term(lo):
            right = own[lo, q] if d == 0 else ring[d - 1, lo]
            if d < 4:
                left = turned[lo].reshape(4 * WIDE, TOKENS)
            else:
                left = turned[lo, pl.ds(2 * a4, 2)].reshape(2 * WIDE, TOKENS)
            return jnp.dot(left, right, preferred_element_type=jnp.float32)

        total = term(0) + term(1)
        if d < 4:
            part[d] = total
        else:
            part4[...] = total

    def held(d):
        if d < 4:
            return part.at[d], zbuf.at[d], 64
        return part4, zbuf4, 32

    arriving = {}

    def z_step(d, s):
        mine, buf, n = held(d)
        for way in (0, 1):
            shift = Z + 4 - s if way else Z - (4 - s)
            base = lax.rem(z + shift, Z) * n
            lo, count = way * (n // 2), n // 2
            if s > 0:
                arriving[d, way, s - 1].wait_recv()
                if s > 1:
                    lo, count = 0, n
                at = pl.ds(pl.multiple_of(base + lo, 8), count)
                mine[at, :] += buf[way, s - 1, lo : lo + count]
                lo, count = 0, n
            copy = remote(
                mine.at[pl.ds(pl.multiple_of(base + lo, 8), count)],
                buf.at[way, s, pl.ds(lo, count)],
                send_z.at[d, way, s], recv_z.at[d, way, s],
                place(y, h, core, low, z_up if way else z_down),
            )
            copy.start()
            arriving[d, way, s] = copy
            sends.append(copy)

    kept = []

    def deliver(d):
        mine, buf, n = held(d)
        here = pl.ds(pl.multiple_of(z * n, 8), n)
        for way in (0, 1):
            arriving[d, way, 3].wait_recv()
        mine[here, :] += buf[0, 3] + buf[1, 3]
        yq = lax.rem(y + Y + jnp.where(core == 0, d, -d), Y)
        t1 = 2 * yq + h
        if d < 4:
            a, kk = lax.div(z, 4), lax.rem(lax.div(z, 2), 2)
            row1, row2 = lax.rem(z, 2) * n, lax.rem(z, 4) * n
        else:
            a, kk = a4, lax.div(z, 4)
            row1, row2 = lax.rem(z, 4) * n, z * n
        dst = direct.at[
            core,
            pl.ds(pl.multiple_of(row1, 8), n),
            pl.ds(pl.multiple_of(low * WIDE, WIDE), WIDE),
        ]
        is_self = (a == h) & (kk == core) & (t1 == tok)
        copy = remote(
            mine.at[here], dst, send_d.at[d, 0], recv_d.at[core],
            place(y, a, kk, lax.div(t1, Z), lax.rem(t1, Z)),
        )
        local = pltpu.make_async_copy(mine.at[here], dst, recv_d.at[core])
        pl.when(jnp.logical_not(is_self))(copy.start)
        pl.when(is_self)(local.start)
        kept.append((jnp.logical_not(is_self), copy))
        if d > 0:
            t2 = 2 * y + a
            copy = remote(
                mine.at[here],
                mirror.at[core, pl.ds(pl.multiple_of(row2, 8), n)],
                send_d.at[d, 1], recv_d.at[core],
                place(yq, h, low, lax.div(t2, Z), lax.rem(t2, Z)),
            )
            copy.start()
            sends.append(copy)

    product(0)
    z_step(0, 0)
    product(1)
    z_step(1, 0)
    ring_wait(2, 0)
    ring_send(3, 0)
    z_step(0, 1)
    product(2)
    z_step(2, 0)
    z_step(1, 1)
    ring_wait(2, 1)
    ring_send(3, 1)
    z_step(0, 2)
    product(3)
    z_step(3, 0)
    z_step(2, 1)
    z_step(1, 2)
    z_step(0, 3)
    ring_wait(3, 0)
    ring_wait(3, 1)
    product(4)
    z_step(4, 0)
    z_step(3, 1)
    z_step(2, 2)
    z_step(1, 3)
    deliver(0)
    z_step(4, 1)
    z_step(3, 2)
    z_step(2, 3)
    deliver(1)
    z_step(4, 2)
    z_step(3, 3)
    deliver(2)
    z_step(4, 3)
    deliver(3)
    deliver(4)

    scale = jnp.float32(1.0 / (TOKENS * 2 * Z))
    y2, h2 = lax.div(tok, 2), lax.rem(tok, 2)
    on_time = jnp.where(y < Y // 2, h == h2, h != h2)
    for i, out in enumerate((out_a, out_g)):
        d = lax.rem((y2 - y if i == 0 else y - y2) + Y, Y)
        straight = (d < 4) | ((d == 4) & on_time)

        @pl.when(straight)
        def _():
            ref = direct.at[i]
            pltpu.make_async_copy(ref, ref, recv_d.at[i]).wait()
            out[...] = direct[i] * scale

        @pl.when(jnp.logical_not(straight))
        def _():
            ref = mirror.at[i]
            pltpu.make_async_copy(ref, ref, recv_d.at[i]).wait()
            out[...] = mirror[i].T * scale

    for copy in sends:
        copy.wait_send()
    for remote_one, copy in kept:
        pl.when(remote_one)(copy.wait_send)


def per_device(activations, gradients):
    vmem, sem = pltpu.VMEM, pltpu.SemaphoreType.DMA
    block = jax.ShapeDtypeStruct((WIDE, 2 * WIDE), jnp.float32)
    return pl.pallas_call(
        kernel,
        out_shape=(block, block),
        in_specs=[pl.BlockSpec(memory_space=pl.ANY)] * 2,
        out_specs=[pl.BlockSpec(memory_space=pltpu.VMEM)] * 2,
        scratch_shapes=[
            vmem((2, 4, TOKENS, WIDE), jnp.bfloat16),
            vmem((2, 4, WIDE, TOKENS), jnp.bfloat16),
            vmem((4, 2, TOKENS, WIDE), jnp.bfloat16),
            vmem((4, 4 * WIDE, WIDE), jnp.float32),
            vmem((2 * WIDE, WIDE), jnp.float32),
            vmem((4, 2, 4, 64, WIDE), jnp.float32),
            vmem((2, 4, 32, WIDE), jnp.float32),
            vmem((2, WIDE, 2 * WIDE), jnp.float32),
            vmem((2, 2 * WIDE, WIDE), jnp.float32),
            sem((7,)), sem((2, 4)),
            sem((4, 2)), sem((4, 2)),
            sem((5, 2, 4)), sem((5, 2, 4)),
            sem((5, 2)), sem((2,)),
        ],
        compiler_params=pltpu.CompilerParams(
            collective_id=0, has_side_effects=True, vmem_limit_bytes=40 * 2**20
        ),
        cost_estimate=pl.CostEstimate(
            flops=2 * 2304 * 1536 * 128, bytes_accessed=2**20, transcendentals=0
        ),
    )(activations, gradients)


def solution(mesh):
    placed = (P("tok", "tp"), P("tok", "tp"))
    return jax.shard_map(
        per_device,
        mesh=mesh,
        in_specs=placed,
        out_specs=(P("tp", "tok"), P("tp", "tok")),
        check_vma=False,
    )
```

time: 383 us -> 69.2 us (0.18)
  the two profiles are of different devices: /device:TPU:8 before, /device:TPU:6 now
where the time goes in v1:
time: 69.2 us; the launch traced here: 69.1 us
  Pallas kernels  65.2 us (94%)
  local copies, waits for them, and re-layouts  3.16 us (5%)
    pallas_call x1, Pallas kernels, per_device(): pl.pallas_call(kernel, out_shape=(block, block), in_specs=[pl.BlockSpec(m...  65.2 us
    unnamed x6, local copies, waits for them, and re-layouts  3.16 us

profile of v1, /device:TPU:6, one launch (start us, length us, event | category | flops | bytes accessed | tf_op | source)
XLA Modules:
  0.0 69.1 jit_solution(5989708543562731425)
XLA Ops:
  0.6 0.0 copy-start
  0.6 0.9 %copy-done = bf16[768,128]{1,0:T(8,128)(2,1)S(1)} copy-done((bf16[768,128]{1,0:T(8,128)(2,1)S(1)}, bf16[768,128]{1,0:T(8,128)(2,1)}, u32[]{:S(2)}) %copy-start) | copy-done | bytes 196632
  1.6 0.0 copy-start.1
  1.6 0.9 %copy-done.1 = bf16[768,128]{1,0:T(8,128)(2,1)S(1)} copy-done((bf16[768,128]{1,0:T(8,128)(2,1)S(1)}, bf16[768,128]{1,0:T(8,128)(2,1)}, u32[]{:S(2)}) %copy-start.1) | copy-done | bytes 196632
  2.5 65.2 %shard_map.41 = (f32[128,256]{1,0:T(8,128)S(1)}, f32[128,256]{1,0:T(8,128)S(1)}) custom-call(bf16[768,128]{1,0:T(8,128)(2,1)S(1)} %copy-done, bf16[768,128]{1,0:T(8,128)(2,1)S(1)} %copy-done.1), custom_call_target="tpu_custom_call" | custom-call | flops 905969664 | bytes 1048576 | tf_op jit(solution)/shard_map/pallas_call | solution.py:289
  67.7 0.7 copy.6
  68.4 0.7 copy.7
Async XLA Ops:
  0.6 0.9 %copy-start = (bf16[768,128]{1,0:T(8,128)(2,1)S(1)}, bf16[768,128]{1,0:T(8,128)(2,1)}, u32[]{:S(2)}) copy-start(bf16[768,128]{1,0:T(8,128)(2,1)} %act.1) | copy-start | bytes 589828
  1.6 0.9 %copy-start.1 = (bf16[768,128]{1,0:T(8,128)(2,1)S(1)}, bf16[768,128]{1,0:T(8,128)(2,1)}, u32[]{:S(2)}) copy-start(bf16[768,128]{1,0:T(8,128)(2,1)} %grad.1) | copy-start | bytes 589828

commit v2 on v1

v2 whole, which is shorter than its diff:
```python
import jax
import jax.numpy as jnp
from jax import lax
from jax.experimental import pallas as pl
from jax.experimental.pallas import tpu as pltpu
from jax.sharding import PartitionSpec as P

TOKENS = 768
WIDE = 128
HALF = TOKENS // 2
CHUNK = 32
Y = 8
Z = 8


def place(y, h, core, low, z):
    return (low * Z + z, (y * 2 + h) * 2 + core)


def kernel(
    act, grad, out_a, out_g,
    own, turned, ring, part, zbuf, direct, mirror,
    send_x, recv_x, send_y, recv_y, send_z, recv_z, send_d, recv_d,
):
    tok, tp = lax.axis_index("tok"), lax.axis_index("tp")
    low, z = lax.div(tok, Z), lax.rem(tok, Z)
    y, h, core = lax.div(tp, 4), lax.rem(lax.div(tp, 2), 2), lax.rem(tp, 2)
    x = 2 * h + low

    def remote(src, dst, send, recv, device):
        return pltpu.make_async_remote_copy(
            src_ref=src, dst_ref=dst, send_sem=send, recv_sem=recv,
            device_id=device, device_id_type=pl.DeviceIdType.MESH,
        )

    def at_x(xx, cc):
        return place(y, lax.div(xx, 2), cc, lax.rem(xx, 2), z)

    x_up, x_down = lax.rem(x + 1, 4), lax.rem(x + 3, 4)
    y_up, y_down = lax.rem(y + 1, Y), lax.rem(y + Y - 1, Y)
    z_up, z_down = lax.rem(z + 1, Z), lax.rem(z + Z - 1, Z)
    sibling = place(y, h, 1 - core, low, z)

    barrier = pltpu.get_barrier_semaphore()
    partners = [sibling]
    partners += [at_x(xx, cc) for xx in (x_up, x_down) for cc in (0, 1)]
    partners += [place(yy, h, core, low, z) for yy in (y_up, y_down)]
    partners += [place(y, h, core, low, zz) for zz in (z_up, z_down)]
    for partner in partners:
        pl.semaphore_signal(
            barrier, inc=1, device_id=partner, device_id_type=pl.DeviceIdType.MESH
        )
    pl.semaphore_wait(barrier, len(partners))

    sends = []
    quarter = 2 * h + core
    pair = 2 * h + 1 - low
    other = lax.rem(x + 3 + 2 * low, 4)
    far = lax.rem(x + 2, 4)
    inputs = (act, grad)

    def piece(ref, part_of):
        return ref.at[pl.ds(part_of * HALF, HALF)]

    for half in (0, 1):
        dst = piece(own.at[low, quarter], half)
        sem = recv_x.at[low, quarter, half]
        for i, ref in enumerate(inputs):
            keep = pltpu.make_async_copy(piece(ref, half), dst, sem)
            give = remote(piece(ref, half), dst, send_x.at[0, half], sem, sibling)
            pl.when(core == i)(keep.start)
            pl.when(core != i)(give.start)
        sends.append(remote(piece(act, half), dst, send_x.at[0, half], sem, sibling))
    first = jnp.where(core == low, other, pair)
    second = jnp.where(core == low, pair, other)

    def x_send(n, half):
        for i, ref in enumerate(inputs):
            copy = remote(
                piece(ref, half), piece(own.at[low, quarter], half),
                send_x.at[1 + 2 * n + i, half], recv_x.at[low, quarter, half],
                at_x(second if n else first, i),
            )
            copy.start()
            sends.append(copy)

    x_send(0, 0)
    x_send(0, 1)

    def slot_of(chip, k):
        return lax.rem(chip, 2), 2 * lax.div(chip, 2) + k

    def arrive(chip, k, half):
        lo, qq = slot_of(chip, k)
        ref = piece(own.at[lo, qq], half)
        pltpu.make_async_copy(ref, ref, recv_x.at[lo, qq, half]).wait()

    def turn(chip):
        for k in (0, 1):
            lo, qq = slot_of(chip, k)
            turned[lo, qq] = own[lo, qq].T

    def pass_on(half, origin, k, to, n):
        lo, qq = slot_of(origin, k)
        ref = piece(own.at[lo, qq], half)
        copy = remote(ref, ref, send_x.at[n, half], recv_x.at[lo, qq, half], at_x(to, core))
        copy.start()
        sends.append(copy)

    q = 2 * h + low
    y_next = jnp.where(core == 0, y_down, y_up)
    groups = (low, 1 - low)

    def ring_piece(step, n, half):
        lo = groups[n]
        if step < 0:
            return piece(own.at[lo, q], half)
        return piece(ring.at[step, lo], half)

    def ring_wait(step, n, half):
        ref = ring_piece(step, n, half)
        pltpu.make_async_copy(ref, ref, recv_y.at[step, groups[n], half]).wait()

    def y_send(step, n, half):
        if step > 0:
            ring_wait(step - 1, n, half)
        copy = remote(
            ring_piece(step - 1, n, half), ring_piece(step, n, half),
            send_y.at[step, n, half], recv_y.at[step, groups[n], half],
            place(y_next, h, core, low, z),
        )
        copy.start()
        sends.append(copy)

    def product(d):
        def term(lo):
            right = own[lo, q] if d == 0 else ring[d - 1, lo]
            left = turned[lo].reshape(4 * WIDE, TOKENS)
            return jnp.dot(left, right, preferred_element_type=jnp.float32)

        part[d] = (term(0) + term(1)).reshape(2, 2 * WIDE, WIDE)

    arriving = {}

    def z_step(d, s):
        mine, buf = part.at[d], zbuf.at[d]
        for way in (0, 1):
            shift = Z + 4 - s if way else Z - (4 - s)
            base = lax.rem(z + shift, Z) * CHUNK
            lo, count = way * (CHUNK // 2), CHUNK // 2
            if s > 0:
                arriving[d, way, s - 1].wait_recv()
                if s > 1:
                    lo, count = 0, CHUNK
                at = pl.ds(pl.multiple_of(base + lo, 8), count)
                mine[:, at, :] += buf[way, s - 1, :, lo : lo + count]
                lo, count = 0, CHUNK
            copy = remote(
                mine.at[:, pl.ds(pl.multiple_of(base + lo, 8), count)],
                buf.at[way, s, :, pl.ds(lo, count)],
                send_z.at[d, way, s], recv_z.at[d, way, s],
                place(y, h, core, low, z_up if way else z_down),
            )
            copy.start()
            arriving[d, way, s] = copy
            sends.append(copy)

    kept = []

    def deliver(d):
        mine, buf = part.at[d], zbuf.at[d]
        here = pl.ds(pl.multiple_of(z * CHUNK, CHUNK), CHUNK)
        for way in (0, 1):
            arriving[d, way, 3].wait_recv()
        mine[:, here, :] += buf[0, 3] + buf[1, 3]
        yq = lax.rem(y + Y + jnp.where(core == 0, d, -d), Y)
        t1 = 2 * yq + h
        kk, row = lax.div(z, 4), lax.rem(z, 4) * CHUNK
        for a in (0, 1):
            dst = direct.at[
                core,
                pl.ds(pl.multiple_of(row, CHUNK), CHUNK),
                pl.ds(pl.multiple_of(low * WIDE, WIDE), WIDE),
            ]
            is_self = (a == h) & (kk == core) & (t1 == tok)
            copy = remote(
                mine.at[a, here], dst, send_d.at[d, a, 0], recv_d.at[core],
                place(y, a, kk, lax.div(t1, Z), lax.rem(t1, Z)),
            )
            local = pltpu.make_async_copy(mine.at[a, here], dst, recv_d.at[core])
            pl.when(jnp.logical_not(is_self))(copy.start)
            pl.when(is_self)(local.start)
            kept.append((jnp.logical_not(is_self), copy))
            if 0 < d < 4:
                t2 = 2 * y + a
                copy = remote(
                    mine.at[a, here],
                    mirror.at[core, here],
                    send_d.at[d, a, 1], recv_d.at[core],
                    place(yq, h, low, lax.div(t2, Z), lax.rem(t2, Z)),
                )
                copy.start()
                sends.append(copy)

    arrive(x, low, 0)
    arrive(x, low, 1)
    arrive(x, 1 - low, 0)
    arrive(x, 1 - low, 1)
    turn(x)
    y_send(0, 0, 0)
    y_send(0, 0, 1)
    arrive(pair, low, 0)
    y_send(0, 1, 0)
    x_send(1, 0)
    pass_on(0, pair, low, other, 5)
    arrive(other, 1 - low, 0)
    pass_on(0, other, 1 - low, pair, 6)
    y_send(1, 0, 0)
    y_send(1, 0, 1)
    arrive(pair, low, 1)
    y_send(0, 1, 1)
    x_send(1, 1)
    pass_on(1, pair, low, other, 5)
    arrive(other, 1 - low, 1)
    pass_on(1, other, 1 - low, pair, 6)
    y_send(1, 1, 0)
    y_send(2, 0, 0)
    y_send(2, 0, 1)
    y_send(1, 1, 1)
    y_send(2, 1, 0)
    y_send(3, 0, 0)
    arrive(other, low, 0)
    arrive(other, low, 1)
    turn(other)
    arrive(pair, 1 - low, 0)
    arrive(pair, 1 - low, 1)
    turn(pair)
    y_send(3, 0, 1)
    y_send(2, 1, 1)
    arrive(far, low, 0)
    arrive(far, low, 1)
    arrive(far, 1 - low, 0)
    arrive(far, 1 - low, 1)
    turn(far)
    product(0)
    z_step(0, 0)
    y_send(3, 1, 0)
    product(1)
    z_step(1, 0)
    product(2)
    z_step(2, 0)
    z_step(0, 1)
    y_send(3, 1, 1)
    z_step(1, 1)
    product(3)
    z_step(3, 0)
    z_step(2, 1)
    z_step(0, 2)
    ring_wait(3, 0, 0)
    ring_wait(3, 0, 1)
    ring_wait(3, 1, 0)
    ring_wait(3, 1, 1)
    product(4)
    z_step(4, 0)
    z_step(1, 2)
    z_step(3, 1)
    z_step(2, 2)
    z_step(0, 3)
    z_step(4, 1)
    z_step(1, 3)
    z_step(3, 2)
    z_step(2, 3)
    early = len(sends)
    deliver(0)
    z_step(4, 2)
    deliver(1)
    z_step(3, 3)
    deliver(2)
    z_step(4, 3)
    deliver(3)
    deliver(4)

    for copy in sends[:early]:
        copy.wait_send()
    scale = jnp.float32(1.0 / (TOKENS * 2 * Z))
    y2 = lax.div(tok, 2)
    for i, out in enumerate((out_a, out_g)):
        d = lax.rem((y2 - y if i == 0 else y - y2) + Y, Y)
        straight = d <= 4

        @pl.when(straight)
        def _():
            ref = direct.at[i]
            pltpu.make_async_copy(ref, ref, recv_d.at[i]).wait()
            out[...] = direct[i] * scale

        @pl.when(jnp.logical_not(straight))
        def _():
            ref = mirror.at[i]
            pltpu.make_async_copy(ref, ref, recv_d.at[i]).wait()
            out[...] = mirror[i].T * scale

    for copy in sends[early:]:
        copy.wait_send()
    for remote_one, copy in kept:
        pl.when(remote_one)(copy.wait_send)


def per_device(activations, gradients):
    vmem, sem = pltpu.VMEM, pltpu.SemaphoreType.DMA
    block = jax.ShapeDtypeStruct((WIDE, 2 * WIDE), jnp.float32)
    return pl.pallas_call(
        kernel,
        out_shape=(block, block),
        in_specs=[pl.BlockSpec(memory_space=pl.ANY)] * 2,
        out_specs=[pl.BlockSpec(memory_space=pltpu.VMEM)] * 2,
        scratch_shapes=[
            vmem((2, 4, TOKENS, WIDE), jnp.bfloat16),
            vmem((2, 4, WIDE, TOKENS), jnp.bfloat16),
            vmem((4, 2, TOKENS, WIDE), jnp.bfloat16),
            vmem((5, 2, 2 * WIDE, WIDE), jnp.float32),
            vmem((5, 2, 4, 2, CHUNK, WIDE), jnp.float32),
            vmem((2, WIDE, 2 * WIDE), jnp.float32),
            vmem((2, 2 * WIDE, WIDE), jnp.float32),
            sem((7, 2)), sem((2, 4, 2)),
            sem((4, 2, 2)), sem((4, 2, 2)),
            sem((5, 2, 4)), sem((5, 2, 4)),
            sem((5, 2, 2)), sem((2,)),
        ],
        compiler_params=pltpu.CompilerParams(
            collective_id=0, has_side_effects=True, vmem_limit_bytes=54840 * 2**10
        ),
        cost_estimate=pl.CostEstimate(
            flops=2 * 2560 * 1536 * 128, bytes_accessed=2**20, transcendentals=0
        ),
    )(activations, gradients)


def solution(mesh):
    placed = (P("tok", "tp"), P("tok", "tp"))
    return jax.shard_map(
        per_device,
        mesh=mesh,
        in_specs=placed,
        out_specs=(P("tp", "tok"), P("tp", "tok")),
        check_vma=False,
    )
```

time: 69.2 us -> 61.3 us (0.89)
  the two profiles are of different devices: /device:TPU:6 before, /device:TPU:7 now
where the time goes in v2:
time: 61.3 us; the launch traced here: 61.2 us
  Pallas kernels  59.2 us (97%)
  local copies, waits for them, and re-layouts  1.31 us (2%)
  between operations  0.64 us (1%)
    pallas_call x1, Pallas kernels, per_device(): pl.pallas_call(kernel, out_shape=(block, block), in_specs=[pl.BlockSpec(m...  59.2 us
    unnamed x2, local copies, waits for them, and re-layouts  1.31 us

profile of v2, /device:TPU:7, one launch (start us, length us, event | category | flops | bytes accessed | tf_op | source)
XLA Modules:
  0.0 61.2 jit_solution(6401335113946448109)
XLA Ops:
  0.6 59.2 %shard_map.41 = (f32[128,256]{1,0:T(8,128)S(1)}, f32[128,256]{1,0:T(8,128)S(1)}) custom-call(bf16[768,128]{1,0:T(8,128)(2,1)} %act.1, bf16[768,128]{1,0:T(8,128)(2,1)} %grad.1), custom_call_target="tpu_custom_call" | custom-call | flops 1006632960 | bytes 1048576 | tf_op jit(solution)/shard_map/pallas_call | solution.py:312
  59.9 0.7 %copy.6 = f32[128,256]{1,0:T(8,128)} copy(f32[128,256]{1,0:T(8,128)S(1)} %get-tuple-element.4) | data formatting | bytes 262144
  60.5 0.7 %copy.7 = f32[128,256]{1,0:T(8,128)} copy(f32[128,256]{1,0:T(8,128)S(1)} %get-tuple-element.5) | data formatting | bytes 262144

commit v3 on v2

--- a/solution.py
+++ b/solution.py
@@ -8,6 +8,7 @@
 TOKENS = 768
 WIDE = 128
 HALF = TOKENS // 2
+NEAR, FAR, BOTH = 0, 1, 2
 CHUNK = 32
 Y = 8
 Z = 8
@@ -19,8 +20,8 @@
 
 def kernel(
     act, grad, out_a, out_g,
-    own, turned, ring, part, zbuf, direct, mirror,
-    send_x, recv_x, send_y, recv_y, send_z, recv_z, send_d, recv_d,
+    own, turned, ring, part, coded, cbuf, direct, mirror,
+    send_x, recv_x, send_y, recv_y, near, send_c, recv_c, send_d, recv_d,
 ):
     tok, tp = lax.axis_index("tok"), lax.axis_index("tp")
     low, z = lax.div(tok, Z), lax.rem(tok, Z)
@@ -132,51 +133,76 @@
         copy.start()
         sends.append(copy)
 
-    def product(d):
+    def rows_of(unit):
+        if unit == BOTH:
+            return 0, 2
+        return (h if unit == NEAR else 1 - h), 1
+
+    def product(d, unit):
+        first, count = rows_of(unit)
+
         def term(lo):
             right = own[lo, q] if d == 0 else ring[d - 1, lo]
-            left = turned[lo].reshape(4 * WIDE, TOKENS)
+            left = turned[lo, pl.ds(2 * first, 2 * count)]
+            left = left.reshape(2 * count * WIDE, TOKENS)
             return jnp.dot(left, right, preferred_element_type=jnp.float32)
 
-        part[d] = (term(0) + term(1)).reshape(2, 2 * WIDE, WIDE)
+        total = term(0) + term(1)
+        part[d, pl.ds(first, count)] = total.reshape(count, 2 * WIDE, WIDE)
 
     arriving = {}
 
-    def z_step(d, s):
-        mine, buf = part.at[d], zbuf.at[d]
+    def greet(n):
+        for way, zz in enumerate((z_up, z_down)):
+            pl.semaphore_signal(
+                near.at[n, way], inc=1, device_id=place(y, h, core, low, zz),
+                device_id_type=pl.DeviceIdType.MESH,
+            )
+
+    def greeted(n):
         for way in (0, 1):
-            shift = Z + 4 - s if way else Z - (4 - s)
-            base = lax.rem(z + shift, Z) * CHUNK
-            lo, count = way * (CHUNK // 2), CHUNK // 2
-            if s > 0:
-                arriving[d, way, s - 1].wait_recv()
-                if s > 1:
-                    lo, count = 0, CHUNK
-                at = pl.ds(pl.multiple_of(base + lo, 8), count)
-                mine[:, at, :] += buf[way, s - 1, :, lo : lo + count]
-                lo, count = 0, CHUNK
+            pl.semaphore_wait(near.at[n, way], 1)
+
+    def scatter(d, unit):
+        side = pl.ds(*rows_of(unit))
+        term = part[d, side] * 0.0625
+        square = term * term
+        power = term * jnp.abs(term) * square * (square * square)
+        coded[d, side] = power.astype(jnp.bfloat16)
+        for o in (4, 3, 5, 2, 6, 1, 7):
+            zz = lax.rem(z + o, Z)
             copy = remote(
-                mine.at[:, pl.ds(pl.multiple_of(base + lo, 8), count)],
-                buf.at[way, s, :, pl.ds(lo, count)],
-                send_z.at[d, way, s], recv_z.at[d, way, s],
-                place(y, h, core, low, z_up if way else z_down),
+                coded.at[d, side, pl.ds(pl.multiple_of(zz * CHUNK, CHUNK), CHUNK)],
+                cbuf.at[d, o - 1, side],
+                send_c.at[d, unit, o - 1], recv_c.at[d, unit, o - 1],
+                place(y, h, core, low, zz),
             )
             copy.start()
-            arriving[d, way, s] = copy
+            arriving[d, unit, o] = copy
             sends.append(copy)
 
+    def gathered(d, unit):
+        side = pl.ds(*rows_of(unit))
+        total = 0.0
+        for o in (1, 7, 2, 6, 3, 5, 4):
+            arriving[d, unit, o].wait_recv()
+            power = cbuf[d, o - 1, side].astype(jnp.float32)
+            root = jnp.sqrt(jnp.sqrt(jnp.sqrt(jnp.abs(power))))
+            total += jnp.where(power < 0.0, -root, root)
+        return total * 16.0
+
     kept = []
 
-    def deliver(d):
-        mine, buf = part.at[d], zbuf.at[d]
+    def deliver(d, unit):
+        first, count = rows_of(unit)
+        mine = part.at[d]
         here = pl.ds(pl.multiple_of(z * CHUNK, CHUNK), CHUNK)
-        for way in (0, 1):
-            arriving[d, way, 3].wait_recv()
-        mine[:, here, :] += buf[0, 3] + buf[1, 3]
+        mine[pl.ds(first, count), here, :] += gathered(d, unit)
         yq = lax.rem(y + Y + jnp.where(core == 0, d, -d), Y)
         t1 = 2 * yq + h
         kk, row = lax.div(z, 4), lax.rem(z, 4) * CHUNK
-        for a in (0, 1):
+        for n in range(count):
+            a = first + n
             dst = direct.at[
                 core,
                 pl.ds(pl.multiple_of(row, CHUNK), CHUNK),
@@ -184,7 +210,7 @@
             ]
             is_self = (a == h) & (kk == core) & (t1 == tok)
             copy = remote(
-                mine.at[a, here], dst, send_d.at[d, a, 0], recv_d.at[core],
+                mine.at[a, here], dst, send_d.at[d, unit + n, 0], recv_d.at[core],
                 place(y, a, kk, lax.div(t1, Z), lax.rem(t1, Z)),
             )
             local = pltpu.make_async_copy(mine.at[a, here], dst, recv_d.at[core])
@@ -196,12 +222,13 @@
                 copy = remote(
                     mine.at[a, here],
                     mirror.at[core, here],
-                    send_d.at[d, a, 1], recv_d.at[core],
+                    send_d.at[d, unit + n, 1], recv_d.at[core],
                     place(yq, h, low, lax.div(t2, Z), lax.rem(t2, Z)),
                 )
                 copy.start()
                 sends.append(copy)
 
+    greet(0)
     arrive(x, low, 0)
     arrive(x, low, 1)
     arrive(x, 1 - low, 0)
@@ -210,6 +237,8 @@
     y_send(0, 0, 0)
     y_send(0, 0, 1)
     arrive(pair, low, 0)
+    greeted(0)
+    greet(1)
     y_send(0, 1, 0)
     x_send(1, 0)
     pass_on(0, pair, low, other, 5)
@@ -222,6 +251,8 @@
     x_send(1, 1)
     pass_on(1, pair, low, other, 5)
     arrive(other, 1 - low, 1)
+    greeted(1)
+    greet(2)
     pass_on(1, other, 1 - low, pair, 6)
     y_send(1, 1, 0)
     y_send(2, 0, 0)
@@ -229,59 +260,51 @@
     y_send(1, 1, 1)
     y_send(2, 1, 0)
     y_send(3, 0, 0)
+    arrive(pair, 1 - low, 0)
+    arrive(pair, 1 - low, 1)
+    turn(pair)
+    greeted(2)
+    product(0, NEAR)
+    scatter(0, NEAR)
+    product(1, NEAR)
+    scatter(1, NEAR)
+    y_send(3, 0, 1)
+    y_send(2, 1, 1)
+    product(2, NEAR)
+    scatter(2, NEAR)
     arrive(other, low, 0)
     arrive(other, low, 1)
     turn(other)
-    arrive(pair, 1 - low, 0)
-    arrive(pair, 1 - low, 1)
-    turn(pair)
-    y_send(3, 0, 1)
-    y_send(2, 1, 1)
     arrive(far, low, 0)
     arrive(far, low, 1)
     arrive(far, 1 - low, 0)
     arrive(far, 1 - low, 1)
     turn(far)
-    product(0)
-    z_step(0, 0)
+    product(0, FAR)
+    scatter(0, FAR)
     y_send(3, 1, 0)
-    product(1)
-    z_step(1, 0)
-    product(2)
-    z_step(2, 0)
-    z_step(0, 1)
     y_send(3, 1, 1)
-    z_step(1, 1)
-    product(3)
-    z_step(3, 0)
-    z_step(2, 1)
-    z_step(0, 2)
+    product(1, FAR)
+    scatter(1, FAR)
+    product(2, FAR)
+    scatter(2, FAR)
+    product(3, BOTH)
+    scatter(3, BOTH)
     ring_wait(3, 0, 0)
     ring_wait(3, 0, 1)
     ring_wait(3, 1, 0)
     ring_wait(3, 1, 1)
-    product(4)
-    z_step(4, 0)
-    z_step(1, 2)
-    z_step(3, 1)
-    z_step(2, 2)
-    z_step(0, 3)
-    z_step(4, 1)
-    z_step(1, 3)
-    z_step(3, 2)
-    z_step(2, 3)
-    early = len(sends)
-    deliver(0)
-    z_step(4, 2)
-    deliver(1)
-    z_step(3, 3)
-    deliver(2)
-    z_step(4, 3)
-    deliver(3)
-    deliver(4)
-
-    for copy in sends[:early]:
-        copy.wait_send()
+    product(4, BOTH)
+    scatter(4, BOTH)
+    deliver(0, NEAR)
+    deliver(1, NEAR)
+    deliver(2, NEAR)
+    deliver(0, FAR)
+    deliver(1, FAR)
+    deliver(2, FAR)
+    deliver(3, BOTH)
+    deliver(4, BOTH)
+
     scale = jnp.float32(1.0 / (TOKENS * 2 * Z))
     y2 = lax.div(tok, 2)
     for i, out in enumerate((out_a, out_g)):
@@ -300,7 +323,7 @@
             pltpu.make_async_copy(ref, ref, recv_d.at[i]).wait()
             out[...] = mirror[i].T * scale
 
-    for copy in sends[early:]:
+    for copy in sends:
         copy.wait_send()
     for remote_one, copy in kept:
         pl.when(remote_one)(copy.wait_send)
@@ -319,13 +342,15 @@
             vmem((2, 4, WIDE, TOKENS), jnp.bfloat16),
             vmem((4, 2, TOKENS, WIDE), jnp.bfloat16),
             vmem((5, 2, 2 * WIDE, WIDE), jnp.float32),
-            vmem((5, 2, 4, 2, CHUNK, WIDE), jnp.float32),
+            vmem((5, 2, 2 * WIDE, WIDE), jnp.bfloat16),
+            vmem((5, 7, 2, CHUNK, WIDE), jnp.bfloat16),
             vmem((2, WIDE, 2 * WIDE), jnp.float32),
             vmem((2, 2 * WIDE, WIDE), jnp.float32),
             sem((7, 2)), sem((2, 4, 2)),
             sem((4, 2, 2)), sem((4, 2, 2)),
-            sem((5, 2, 4)), sem((5, 2, 4)),
-            sem((5, 2, 2)), sem((2,)),
+            pltpu.SemaphoreType.REGULAR((3, 2)),
+            sem((5, 3, 7)), sem((5, 3, 7)),
+            sem((5, 4, 2)), sem((2,)),
         ],
         compiler_params=pltpu.CompilerParams(
             collective_id=0, has_side_effects=True, vmem_limit_bytes=54840 * 2**10

time: 61.3 us -> 57.4 us (0.936)
  Pallas kernels: 59.2 us -> 55.3 us
    pallas_call x1, Pallas kernels: 59.2 us -> 55.3 us  [per_device(): pl.pallas_call(kernel, out_shape=(block, block), in_specs=[pl.BlockSpec(m...]
where the time goes in v3:
time: 57.4 us; the launch traced here: 57.2 us
  Pallas kernels  55.3 us (96%)
  local copies, waits for them, and re-layouts  1.31 us (2%)
  between operations  0.64 us (1%)
    pallas_call x1, Pallas kernels, per_device(): pl.pallas_call(kernel, out_shape=(block, block), in_specs=[pl.BlockSpec(m...  55.3 us
    unnamed x2, local copies, waits for them, and re-layouts  1.31 us

profile of v3, /device:TPU:7, one launch (start us, length us, event | category | flops | bytes accessed | tf_op | source)
XLA Modules:
  0.0 57.2 jit_solution(5311047195237631619)
XLA Ops:
  0.6 55.3 %shard_map.41 = (f32[128,256]{1,0:T(8,128)S(1)}, f32[128,256]{1,0:T(8,128)S(1)}) custom-call(bf16[768,128]{1,0:T(8,128)(2,1)} %act.1, bf16[768,128]{1,0:T(8,128)(2,1)} %grad.1), custom_call_target="tpu_custom_call" | custom-call | flops 1006632960 | bytes 1048576 | tf_op jit(solution)/shard_map/pallas_call | solution.py:335
  55.9 0.7 %copy.6 = f32[128,256]{1,0:T(8,128)} copy(f32[128,256]{1,0:T(8,128)S(1)} %get-tuple-element.4) | data formatting | bytes 262144
  56.6 0.7 %copy.7 = f32[128,256]{1,0:T(8,128)} copy(f32[128,256]{1,0:T(8,128)S(1)} %get-tuple-element.5) | data formatting | bytes 262144

commit v4 on v3

--- a/solution.py
+++ b/solution.py
@@ -45,7 +45,7 @@
     barrier = pltpu.get_barrier_semaphore()
     partners = [sibling]
     partners += [at_x(xx, cc) for xx in (x_up, x_down) for cc in (0, 1)]
-    partners += [place(yy, h, core, low, z) for yy in (y_up, y_down)]
+    partners += [place(yy, h, cc, low, z) for yy in (y_up, y_down) for cc in (0, 1)]
     partners += [place(y, h, core, low, zz) for zz in (z_up, z_down)]
     for partner in partners:
         pl.semaphore_signal(
@@ -53,7 +53,6 @@
         )
     pl.semaphore_wait(barrier, len(partners))
 
-    sends = []
     quarter = 2 * h + core
     pair = 2 * h + 1 - low
     other = lax.rem(x + 3 + 2 * low, 4)
@@ -68,10 +67,9 @@
         sem = recv_x.at[low, quarter, half]
         for i, ref in enumerate(inputs):
             keep = pltpu.make_async_copy(piece(ref, half), dst, sem)
-            give = remote(piece(ref, half), dst, send_x.at[0, half], sem, sibling)
+            give = remote(piece(ref, half), dst, send_x.at[0], sem, sibling)
             pl.when(core == i)(keep.start)
             pl.when(core != i)(give.start)
-        sends.append(remote(piece(act, half), dst, send_x.at[0, half], sem, sibling))
     first = jnp.where(core == low, other, pair)
     second = jnp.where(core == low, pair, other)
 
@@ -79,12 +77,20 @@
         for i, ref in enumerate(inputs):
             copy = remote(
                 piece(ref, half), piece(own.at[low, quarter], half),
-                send_x.at[1 + 2 * n + i, half], recv_x.at[low, quarter, half],
+                send_x.at[1], recv_x.at[low, quarter, half],
                 at_x(second if n else first, i),
             )
             copy.start()
-            sends.append(copy)
-
+
+    kept = []
+    for half in (0, 1):
+        for i, ref in enumerate(inputs):
+            copy = remote(
+                piece(ref, half), piece(ring.at[0, low], half),
+                send_y.at[0], recv_y.at[0, low, half],
+                place(y_up if i else y_down, h, i, low, z),
+            )
+            pl.when(core == low)(copy.start)
     x_send(0, 0)
     x_send(0, 1)
 
@@ -104,9 +110,8 @@
     def pass_on(half, origin, k, to, n):
         lo, qq = slot_of(origin, k)
         ref = piece(own.at[lo, qq], half)
-        copy = remote(ref, ref, send_x.at[n, half], recv_x.at[lo, qq, half], at_x(to, core))
+        copy = remote(ref, ref, send_x.at[2], recv_x.at[lo, qq, half], at_x(to, core))
         copy.start()
-        sends.append(copy)
 
     q = 2 * h + low
     y_next = jnp.where(core == 0, y_down, y_up)
@@ -127,11 +132,10 @@
             ring_wait(step - 1, n, half)
         copy = remote(
             ring_piece(step - 1, n, half), ring_piece(step, n, half),
-            send_y.at[step, n, half], recv_y.at[step, groups[n], half],
+            send_y.at[min(step, 1) + 1], recv_y.at[step, groups[n], half],
             place(y_next, h, core, low, z),
         )
         copy.start()
-        sends.append(copy)
 
     def rows_of(unit):
         if unit == BOTH:
@@ -149,8 +153,6 @@
 
         total = term(0) + term(1)
         part[d, pl.ds(first, count)] = total.reshape(count, 2 * WIDE, WIDE)
-
-    arriving = {}
 
     def greet(n):
         for way, zz in enumerate((z_up, z_down)):
@@ -174,24 +176,22 @@
             copy = remote(
                 coded.at[d, side, pl.ds(pl.multiple_of(zz * CHUNK, CHUNK), CHUNK)],
                 cbuf.at[d, o - 1, side],
-                send_c.at[d, unit, o - 1], recv_c.at[d, unit, o - 1],
+                send_c.at[0], recv_c.at[d, unit],
                 place(y, h, core, low, zz),
             )
             copy.start()
-            arriving[d, unit, o] = copy
-            sends.append(copy)
 
     def gathered(d, unit):
         side = pl.ds(*rows_of(unit))
+        terms = cbuf.at[d, :, side]
+        pltpu.make_async_copy(terms, terms, recv_c.at[d, unit]).wait()
         total = 0.0
-        for o in (1, 7, 2, 6, 3, 5, 4):
-            arriving[d, unit, o].wait_recv()
+        for o in range(1, Z):
             power = cbuf[d, o - 1, side].astype(jnp.float32)
             root = jnp.sqrt(jnp.sqrt(jnp.sqrt(jnp.abs(power))))
             total += jnp.where(power < 0.0, -root, root)
         return total * 16.0
 
-    kept = []
 
     def deliver(d, unit):
         first, count = rows_of(unit)
@@ -210,7 +210,7 @@
             ]
             is_self = (a == h) & (kk == core) & (t1 == tok)
             copy = remote(
-                mine.at[a, here], dst, send_d.at[d, unit + n, 0], recv_d.at[core],
+                mine.at[a, here], dst, send_d.at[2 * d + unit % 2 + n], recv_d.at[core],
                 place(y, a, kk, lax.div(t1, Z), lax.rem(t1, Z)),
             )
             local = pltpu.make_async_copy(mine.at[a, here], dst, recv_d.at[core])
@@ -222,11 +222,10 @@
                 copy = remote(
                     mine.at[a, here],
                     mirror.at[core, here],
-                    send_d.at[d, unit + n, 1], recv_d.at[core],
+                    send_d.at[10], recv_d.at[core],
                     place(yq, h, low, lax.div(t2, Z), lax.rem(t2, Z)),
                 )
                 copy.start()
-                sends.append(copy)
 
     greet(0)
     arrive(x, low, 0)
@@ -234,8 +233,6 @@
     arrive(x, 1 - low, 0)
     arrive(x, 1 - low, 1)
     turn(x)
-    y_send(0, 0, 0)
-    y_send(0, 0, 1)
     arrive(pair, low, 0)
     greeted(0)
     greet(1)
@@ -323,8 +320,17 @@
             pltpu.make_async_copy(ref, ref, recv_d.at[i]).wait()
             out[...] = mirror[i].T * scale
 
-    for copy in sends:
-        copy.wait_send()
+    def all_left(ref, sem):
+        pltpu.make_async_copy(ref, ref, sem).wait()
+
+    all_left(own.at[0, 0], send_x.at[0])
+    all_left(own.at[0], send_x.at[1])
+    all_left(own.at[0, pl.ds(0, 2)], send_x.at[2])
+    pl.when(core == low)(lambda: all_left(ring.at[0], send_y.at[0]))
+    all_left(ring.at[0, 0], send_y.at[1])
+    all_left(ring.at[pl.ds(0, 3)], send_y.at[2])
+    all_left(cbuf, send_c.at[0])
+    all_left(mirror.at[0, pl.ds(0, 6 * CHUNK)], send_d.at[10])
     for remote_one, copy in kept:
         pl.when(remote_one)(copy.wait_send)
 
@@ -346,11 +352,11 @@
             vmem((5, 7, 2, CHUNK, WIDE), jnp.bfloat16),
             vmem((2, WIDE, 2 * WIDE), jnp.float32),
             vmem((2, 2 * WIDE, WIDE), jnp.float32),
-            sem((7, 2)), sem((2, 4, 2)),
-            sem((4, 2, 2)), sem((4, 2, 2)),
+            sem((3,)), sem((2, 4, 2)),
+            sem((3,)), sem((4, 2, 2)),
             pltpu.SemaphoreType.REGULAR((3, 2)),
-            sem((5, 3, 7)), sem((5, 3, 7)),
-            sem((5, 4, 2)), sem((2,)),
+            sem((1,)), sem((5, 3)),
+            sem((11,)), sem((2,)),
         ],
         compiler_params=pltpu.CompilerParams(
             collective_id=0, has_side_effects=True, vmem_limit_bytes=54840 * 2**10

time: 57.4 us -> 54.3 us (0.946)
  Pallas kernels: 55.3 us -> 52.2 us
    pallas_call x1, Pallas kernels: 55.3 us -> 52.2 us  [per_device(): pl.pallas_call(kernel, out_shape=(block, block), in_specs=[pl.BlockSpec(m...]
where the time goes in v4:
time: 54.3 us; the launch traced here: 54.2 us
  Pallas kernels  52.2 us (96%)
  local copies, waits for them, and re-layouts  1.31 us (2%)
  between operations  0.64 us (1%)
    pallas_call x1, Pallas kernels, per_device(): pl.pallas_call(kernel, out_shape=(block, block), in_specs=[pl.BlockSpec(m...  52.2 us
    unnamed x2, local copies, waits for them, and re-layouts  1.31 us

profile of v4, /device:TPU:7, one launch (start us, length us, event | category | flops | bytes accessed | tf_op | source)
XLA Modules:
  0.0 54.2 jit_solution(7934880480715372566)
XLA Ops:
  0.6 52.2 %shard_map.41 = (f32[128,256]{1,0:T(8,128)S(1)}, f32[128,256]{1,0:T(8,128)S(1)}) custom-call(bf16[768,128]{1,0:T(8,128)(2,1)} %act.1, bf16[768,128]{1,0:T(8,128)(2,1)} %grad.1), custom_call_target="tpu_custom_call" | custom-call | flops 1006632960 | bytes 1048576 | tf_op jit(solution)/shard_map/pallas_call | solution.py:341
  52.9 0.7 %copy.6 = f32[128,256]{1,0:T(8,128)} copy(f32[128,256]{1,0:T(8,128)S(1)} %get-tuple-element.4) | data formatting | bytes 262144
  53.5 0.7 %copy.7 = f32[128,256]{1,0:T(8,128)} copy(f32[128,256]{1,0:T(8,128)S(1)} %get-tuple-element.5) | data formatting | bytes 262144

commit v5 on v4

--- a/solution.py
+++ b/solution.py
@@ -151,7 +151,11 @@
             left = left.reshape(2 * count * WIDE, TOKENS)
             return jnp.dot(left, right, preferred_element_type=jnp.float32)
 
-        total = term(0) + term(1)
+        total = term(groups[0])
+        if d == 4:
+            ring_wait(3, 1, 0)
+            ring_wait(3, 1, 1)
+        total += term(groups[1])
         part[d, pl.ds(first, count)] = total.reshape(count, 2 * WIDE, WIDE)
 
     def greet(n):
@@ -176,7 +180,7 @@
             copy = remote(
                 coded.at[d, side, pl.ds(pl.multiple_of(zz * CHUNK, CHUNK), CHUNK)],
                 cbuf.at[d, o - 1, side],
-                send_c.at[0], recv_c.at[d, unit],
+                send_c.at[0], recv_c.at[d + 5 * (unit % 2)],
                 place(y, h, core, low, zz),
             )
             copy.start()
@@ -184,7 +188,7 @@
     def gathered(d, unit):
         side = pl.ds(*rows_of(unit))
         terms = cbuf.at[d, :, side]
-        pltpu.make_async_copy(terms, terms, recv_c.at[d, unit]).wait()
+        pltpu.make_async_copy(terms, terms, recv_c.at[d + 5 * (unit % 2)]).wait()
         total = 0.0
         for o in range(1, Z):
             power = cbuf[d, o - 1, side].astype(jnp.float32)
@@ -289,17 +293,15 @@
     scatter(3, BOTH)
     ring_wait(3, 0, 0)
     ring_wait(3, 0, 1)
-    ring_wait(3, 1, 0)
-    ring_wait(3, 1, 1)
     product(4, BOTH)
     scatter(4, BOTH)
+    deliver(2, NEAR)
+    deliver(2, FAR)
+    deliver(1, NEAR)
+    deliver(1, FAR)
+    deliver(3, BOTH)
     deliver(0, NEAR)
-    deliver(1, NEAR)
-    deliver(2, NEAR)
     deliver(0, FAR)
-    deliver(1, FAR)
-    deliver(2, FAR)
-    deliver(3, BOTH)
     deliver(4, BOTH)
 
     scale = jnp.float32(1.0 / (TOKENS * 2 * Z))
@@ -355,7 +357,7 @@
             sem((3,)), sem((2, 4, 2)),
             sem((3,)), sem((4, 2, 2)),
             pltpu.SemaphoreType.REGULAR((3, 2)),
-            sem((1,)), sem((5, 3)),
+            sem((1,)), sem((8,)),
             sem((11,)), sem((2,)),
         ],
         compiler_params=pltpu.CompilerParams(

time: 54.3 us -> 54 us (level)
  no operation moved by 1% of the time
where the time goes in v5:
time: 54 us; the launch traced here: 53.9 us
  Pallas kernels  51.9 us (96%)
  local copies, waits for them, and re-layouts  1.31 us (2%)
  between operations  0.64 us (1%)
    pallas_call x1, Pallas kernels, per_device(): pl.pallas_call(kernel, out_shape=(block, block), in_specs=[pl.BlockSpec(m...  51.9 us
    unnamed x2, local copies, waits for them, and re-layouts  1.31 us

profile of v5, /device:TPU:7, one launch (start us, length us, event | category | flops | bytes accessed | tf_op | source)
XLA Modules:
  0.0 53.9 jit_solution(15064153858956218887)
XLA Ops:
  0.6 51.9 %shard_map.41 = (f32[128,256]{1,0:T(8,128)S(1)}, f32[128,256]{1,0:T(8,128)S(1)}) custom-call(bf16[768,128]{1,0:T(8,128)(2,1)} %act.1, bf16[768,128]{1,0:T(8,128)(2,1)} %grad.1), custom_call_target="tpu_custom_call" | custom-call | flops 1006632960 | bytes 1048576 | tf_op jit(solution)/shard_map/pallas_call | solution.py:343
  52.6 0.7 %copy.6 = f32[128,256]{1,0:T(8,128)} copy(f32[128,256]{1,0:T(8,128)S(1)} %get-tuple-element.4) | data formatting | bytes 262144
  53.2 0.7 %copy.7 = f32[128,256]{1,0:T(8,128)} copy(f32[128,256]{1,0:T(8,128)S(1)} %get-tuple-element.5) | data formatting | bytes 262144

commit v6 on v5

--- a/solution.py
+++ b/solution.py
@@ -207,6 +207,17 @@
         kk, row = lax.div(z, 4), lax.rem(z, 4) * CHUNK
         for n in range(count):
             a = first + n
+            if 0 < d < 4:
+                t2 = 2 * y + a
+                copy = remote(
+                    mine.at[a, here],
+                    mirror.at[core, here],
+                    send_d.at[10], recv_d.at[core],
+                    place(yq, h, low, lax.div(t2, Z), lax.rem(t2, Z)),
+                )
+                copy.start()
+        for n in range(count):
+            a = first + n
             dst = direct.at[
                 core,
                 pl.ds(pl.multiple_of(row, CHUNK), CHUNK),
@@ -221,15 +232,6 @@
             pl.when(jnp.logical_not(is_self))(copy.start)
             pl.when(is_self)(local.start)
             kept.append((jnp.logical_not(is_self), copy))
-            if 0 < d < 4:
-                t2 = 2 * y + a
-                copy = remote(
-                    mine.at[a, here],
-                    mirror.at[core, here],
-                    send_d.at[10], recv_d.at[core],
-                    place(yq, h, low, lax.div(t2, Z), lax.rem(t2, Z)),
-                )
-                copy.start()
 
     greet(0)
     arrive(x, low, 0)

time: 54 us -> 54 us (level)
  no operation moved by 1% of the time
where the time goes in v6:
time: 54 us; the launch traced here: 53.8 us
  Pallas kernels  51.9 us (96%)
  local copies, waits for them, and re-layouts  1.31 us (2%)
  between operations  0.64 us (1%)
    pallas_call x1, Pallas kernels, per_device(): pl.pallas_call(kernel, out_shape=(block, block), in_specs=[pl.BlockSpec(m...  51.9 us
    unnamed x2, local copies, waits for them, and re-layouts  1.31 us

profile of v6, /device:TPU:7, one launch (start us, length us, event | category | flops | bytes accessed | tf_op | source)
XLA Modules:
  0.0 53.8 jit_solution(4520516999052651958)
XLA Ops:
  0.6 51.9 %shard_map.41 = (f32[128,256]{1,0:T(8,128)S(1)}, f32[128,256]{1,0:T(8,128)S(1)}) custom-call(bf16[768,128]{1,0:T(8,128)(2,1)} %act.1, bf16[768,128]{1,0:T(8,128)(2,1)} %grad.1), custom_call_target="tpu_custom_call" | custom-call | flops 1006632960 | bytes 1048576 | tf_op jit(solution)/shard_map/pallas_call | solution.py:345
  52.5 0.7 %copy.6 = f32[128,256]{1,0:T(8,128)} copy(f32[128,256]{1,0:T(8,128)S(1)} %get-tuple-element.4) | data formatting | bytes 262144
  53.2 0.7 %copy.7 = f32[128,256]{1,0:T(8,128)} copy(f32[128,256]{1,0:T(8,128)S(1)} %get-tuple-element.5) | data formatting | bytes 262144
